TPU v7x, 32 devices: a whole 2x2x4 slice. The times are simulated.
32 devices in a mesh: pos: 8 (over y, x, core), tile: 4 (over z).
Axes of the slice: x: 2, y: 2, z: 4, core: 2. Of those that a mesh axis runs over, the one named last changes fastest.
Arguments:
- obj_tiles: bfloat16 [192, 4, 4096], P('pos'), may hold values from -4.1875 to 4.1875
- tile_map: int32 [32, 6], replicated, may hold values from 0 to 191, as said below
- offsets: int32 [32, 2], replicated, may hold values from 1 to 1919, as said below
- probe: float32 [2, 128, 128], replicated, may hold values from -6 to 6
- intens: float32 [32, 128, 128], P(('pos', 'tile')), may hold values from 0.05 to 2
Outputs:
- obj_grad: float32 [192, 4, 4096], P('pos')
- probe_grad: float32 [2, 128, 128], replicated
Inputs may be any that keep to these rules, and one draw needn't show every extreme that they name: tile_map holds every storage index once. A tile's owner is its storage index // 24; the owner depends only on the tile row mod 8 and the tile column mod 1, and different such classes have different owners. `offsets`: every patch lies inside the window, and neither its row nor its column offset is a multiple of 64.
All inputs are finite; a program needn't handle non-finite values.
Results may differ from a plain program's by a relative error of at most 0.0023.
Values may be sent and summed in bfloat16 or wider, within the bound.
A program may use at most 64 MiB of HBM per device.

v0:
```python
import math

import jax
import jax.numpy as jnp
from jax import lax
from jax.sharding import PartitionSpec as P

TS = 64
OWN_R = 8


def matmul_hi(left_op, right_op):
    return jnp.dot(
        left_op, right_op, precision=lax.Precision.HIGHEST, preferred_element_type=jnp.float32
    )


def spectral_tables(width_px):
    positions = jnp.arange(width_px, dtype=jnp.int32)
    phase_idx = positions[:, None] * positions[None, :] % width_px
    angles = phase_idx.astype(jnp.float32) * (2.0 * math.pi / width_px)
    norm_factor = 1.0 / math.sqrt(width_px)
    return (jnp.cos(angles) * norm_factor, -jnp.sin(angles) * norm_factor)


def complex_matmul(left_re, left_im, right_re, right_im):
    out_re = matmul_hi(left_re, right_re) - matmul_hi(left_im, right_im)
    out_im = matmul_hi(left_re, right_im) + matmul_hi(left_im, right_re)
    return (out_re, out_im)


def propagation_matrix(width_px, fwd_re, fwd_im, sign_val):
    positions = jnp.arange(width_px, dtype=jnp.int32)
    centred = (positions + width_px // 2) % width_px - width_px // 2
    angles = (centred * centred).astype(jnp.float32) * (-0.2 / width_px) * sign_val
    phase_re = jnp.cos(angles)[:, None]
    phase_im = jnp.sin(angles)[:, None]
    scaled_re = phase_re * fwd_re - phase_im * fwd_im
    scaled_im = phase_re * fwd_im + phase_im * fwd_re
    return complex_matmul(fwd_re, -fwd_im, scaled_re, scaled_im)


def transform(part_re, part_im, table_re, table_im):
    mid_re, mid_im = complex_matmul(part_re, part_im, table_re, table_im)
    return complex_matmul(table_re, table_im, mid_re, mid_im)


def product(left_re, left_im, right_re, right_im):
    return (left_re * right_re - left_im * right_im, left_re * right_im + left_im * right_re)


def per_device(obj_tiles, tile_map, offsets, probe, intens):
    owners = lax.axis_size("pos")
    layers = lax.axis_size("tile")
    me_pos = lax.axis_index("pos")
    me_tile = lax.axis_index("tile")
    tiles_dev = obj_tiles.shape[0]
    tile_edge = TS
    width_px = probe.shape[-1]
    tile_span = width_px // tile_edge + 1
    cols_own = owners // OWN_R
    cols_cap = (tile_span + cols_own - 1) // cols_own
    slots = (tile_span + OWN_R - 1) // OWN_R * cols_cap
    span_idx = jnp.arange(tile_span, dtype=jnp.int32)
    slot_grid = (span_idx[:, None] // OWN_R * cols_cap + span_idx[None, :] // cols_own).reshape(-1)

    def footprint(corner):
        row_ids = corner[0] // tile_edge + span_idx
        col_ids = corner[1] // tile_edge + span_idx
        store_id = tile_map[row_ids[:, None], col_ids[None, :]].reshape(-1)
        owner_id = store_id // tiles_dev
        return (owner_id, store_id - owner_id * tiles_dev)

    by_device = offsets.reshape(owners, layers, 2)
    peer_corners = lax.dynamic_index_in_dim(by_device, me_tile, 1, keepdims=False)
    peer_owner, peer_local = jax.vmap(footprint)(peer_corners)
    slot_ids = jnp.arange(slots, dtype=jnp.int32)
    matches = (peer_owner == me_pos)[:, :, None] & (
        slot_grid[None, :, None] == slot_ids[None, None, :]
    )
    send_local = jnp.sum(jnp.where(matches, peer_local[:, :, None], 0), axis=1)
    send_live = jnp.any(matches, axis=1)
    chosen = jnp.where(
        send_live[:, :, None, None], obj_tiles[send_local], jnp.zeros((), obj_tiles.dtype)
    )
    my_corner = lax.dynamic_index_in_dim(offsets, me_pos * layers + me_tile, 0, keepdims=False)
    my_owner, my_local = footprint(my_corner)
    flat_slot = my_owner * slots + slot_grid
    inner_y = my_corner[0] % tile_edge
    inner_x = my_corner[1] % tile_edge
    zero_idx = jnp.zeros((), jnp.int32)
    fwd_re, fwd_im = spectral_tables(width_px)
    ahead_re, ahead_im = propagation_matrix(width_px, fwd_re, fwd_im, 1.0)
    behind_re, behind_im = propagation_matrix(width_px, fwd_re, fwd_im, -1.0)
    probe_re = probe[0]
    probe_im = probe[1]
    received = lax.all_to_all(chosen, "pos", split_axis=0, concat_axis=0, tiled=True)
    n_comps = received.shape[2]
    pieces = received.reshape(owners * slots, n_comps, tile_edge * tile_edge)[flat_slot]
    region = pieces.reshape(tile_span, tile_span, n_comps, tile_edge, tile_edge).transpose(
        2, 0, 3, 1, 4
    )
    region = region.reshape(n_comps, tile_span * tile_edge, tile_span * tile_edge)
    patch_px = lax.dynamic_slice(
        region, (zero_idx, inner_y, inner_x), (n_comps, width_px, width_px)
    )
    fetched = patch_px.astype(jnp.float32)
    entry_patch = fetched[:2]
    leaving = fetched[2:]
    first_re, first_im = product(probe_re, probe_im, entry_patch[0], entry_patch[1])
    spread_re, spread_im = transform(first_re, first_im, ahead_re, ahead_im)
    second_re, second_im = product(spread_re, spread_im, leaving[0], leaving[1])
    far_re, far_im = transform(second_re, second_im, fwd_re, fwd_im)
    excess = far_re * far_re + far_im * far_im - intens[0]
    back_re, back_im = transform(excess * far_re, excess * far_im, fwd_re, -fwd_im)
    exit_re, exit_im = product(spread_re, -spread_im, back_re, back_im)
    mid_re, mid_im = product(leaving[0], -leaving[1], back_re, back_im)
    inner_re, inner_im = transform(mid_re, mid_im, behind_re, behind_im)
    entry_re, entry_im = product(probe_re, -probe_im, inner_re, inner_im)
    grad_re, grad_im = product(entry_patch[0], -entry_patch[1], inner_re, inner_im)
    patch_grad = jnp.stack([entry_re, entry_im, exit_re, exit_im]).astype(jnp.bfloat16)
    region = jnp.zeros((4, tile_span * tile_edge, tile_span * tile_edge), jnp.bfloat16)
    region = lax.dynamic_update_slice(region, patch_grad, (zero_idx, inner_y, inner_x))
    pieces = region.reshape(4, tile_span, tile_edge, tile_span, tile_edge).transpose(1, 3, 0, 2, 4)
    pieces = pieces.reshape(tile_span * tile_span, 4, tile_edge * tile_edge)
    outgoing = (
        jnp.zeros((owners * slots, 4, tile_edge * tile_edge), jnp.bfloat16)
        .at[flat_slot]
        .set(pieces)
    )
    outgoing = outgoing.reshape(owners, slots, 4, tile_edge * tile_edge)
    returned = lax.all_to_all(outgoing, "pos", split_axis=0, concat_axis=0, tiled=True)
    tile_ids = jnp.arange(tiles_dev, dtype=jnp.int32)
    selector = (
        (send_local.reshape(-1)[None, :] == tile_ids[:, None]) & send_live.reshape(-1)[None, :]
    ).astype(jnp.bfloat16)
    local_sum = jnp.dot(
        selector,
        returned.reshape(owners * slots, 4 * tile_edge * tile_edge),
        preferred_element_type=jnp.float32,
    )
    probe_part = jnp.stack([grad_re, grad_im])
    tile_total, probe_layer = lax.psum((local_sum, probe_part), "tile")
    probe_total = lax.psum(probe_layer, "pos")
    return (tile_total.reshape(tiles_dev, 4, tile_edge * tile_edge), probe_total)


def solution(mesh):
    in_specs = (P("pos", None, None), P(), P(), P(), P(("pos", "tile"), None, None))
    out_specs = (P("pos", None, None), P())
    return jax.shard_map(
        per_device, mesh=mesh, in_specs=in_specs, out_specs=out_specs, check_vma=False
    )
```

profile of v0, /device:TPU:0, one launch (start us, length us, event | category | flops | bytes accessed | tf_op | source)
XLA Modules:
  0.0 213.4 jit_solution(1281983515651094889)
XLA Ops:
  7.2 0.8 constant_dynamic-slice_fusion
  8.0 0.5 fusion.188
  10.5 0.8 reshape.369
  11.8 1.3 gather_fusion
  14.7 1.2 gather_fusion.2
  15.9 1.3 broadcast_select_fusion
  17.2 5.2 %all-to-all-start = ((bf16[8,3,4,4096]{3,2,1,0:T(4,128)(2,1)}), bf16[8,3,4,4096]{3,2,1,0:T(4,128)(2,1)S(1)}, u32[]{:S(2)}, u32[]{:S(2)}) async-start(bf16[8,3,4,4096]{3,2,1,0:T(4,128)(2,1)} %broadcast_select_fusion), calls=%async_computation | async-start | bytes 1572864 | tf_op jit(solution)/shard_map/all_to_all | solution.py:97
  27.2 0.7 gather_fusion.1
  27.9 0.5 convolution_add_fusion.9
  30.0 5.0 %all-to-all-done = bf16[8,3,4,4096]{3,2,1,0:T(4,128)(2,1)S(1)} async-done(((bf16[8,3,4,4096]{3,2,1,0:T(4,128)(2,1)}), bf16[8,3,4,4096]{3,2,1,0:T(4,128)(2,1)S(1)}, u32[]{:S(2)}, u32[]{:S(2)}) %all-to-all-start) | async-done | bytes 786464 | tf_op jit(solution)/shard_map/all_to_all | solution.py:97
  34.9 0.8 gather_fusion.3
  36.2 0.5 copy.17
  46.1 0.7 multiply_add_fusion
  48.6 2.9 %dynamic_update_slice.3 = bf16[4,192,192]{2,1,0:T(8,128)(2,1)S(1)} dynamic-update-slice(bf16[4,192,192]{2,1,0:T(8,128)(2,1)S(1)} %broadcast_in_dim.43, bf16[4,128,128]{2,1,0:T(8,128)(2,1)S(1)} %pad_maximum_fusion, s32[]{:T(128)} %constant.149.clone.1, s32[]{:T(128)S(6)} %select_n.270, s32[]{:T(128)S(6)} %select_n.272) | dynamic-update-slice | bytes 262148 | tf_op jit(solution)/shard_map/dynamic_update_slice | solution.py:123
  52.2 1.2 broadcast_in_dim.40
  53.5 2.4 %scatter_fusion = bf16[24,4,4096]{2,1,0:T(4,128)(2,1)} fusion(bf16[24,4,4096]{2,1,0:T(4,128)(2,1)} %broadcast_in_dim.40, s32[9]{0:T(128)S(1)} %fusion.83, bf16[9,4,4096]{2,1,0:T(4,128)(2,1)S(1)} %reshape.411), kind=kCustom, calls=%fused_computation.4 | custom fusion | bytes 884772 | tf_op jit(solution)/shard_map/scatter | solution.py:129
  55.9 3.5 %all-to-all-start.1 = ((bf16[8,3,4,4096]{3,2,1,0:T(4,128)(2,1)}), bf16[8,3,4,4096]{3,2,1,0:T(4,128)(2,1)S(1)}, u32[]{:S(2)}, u32[]{:S(2)}) async-start(bf16[8,3,4,4096]{3,2,1,0:T(4,128)(2,1)} %bitcast.23), calls=%async_computation.1 | async-start | bytes 1572864 | tf_op jit(solution)/shard_map/all_to_all | solution.py:132
  59.7 0.7 pad_maximum_fusion.1
  60.4 11.6 %all-to-all-done.1 = bf16[8,3,4,4096]{3,2,1,0:T(4,128)(2,1)S(1)} async-done(((bf16[8,3,4,4096]{3,2,1,0:T(4,128)(2,1)}), bf16[8,3,4,4096]{3,2,1,0:T(4,128)(2,1)S(1)}, u32[]{:S(2)}, u32[]{:S(2)}) %all-to-all-start.1) | async-done | bytes 786464 | tf_op jit(solution)/shard_map/all_to_all | solution.py:132
  72.8 2.2 %reshape.378 = f32[24,4,4096]{2,1,0:T(4,128)} reshape(f32[24,16384]{1,0:T(8,128)S(1)} %fusion.41) | data formatting | bytes 3145728 | tf_op jit(solution)/shard_map/reshape | solution.py:145
  75.0 73.1 %all-reduce.6.cloned.1.call-done = (f32[24,4,4096]{2,1,0:T(4,128)}, f32[2,128,128]{2,1,0:T(8,128)}) async-done(((f32[24,4,4096]{2,1,0:T(4,128)}, f32[2,128,128]{2,1,0:T(8,128)}), (f32[24,4,4096]{2,1,0:T(4,128)}, f32[2,128,128]{2,1,0:T(8,128)})) %all-reduce.6.cloned.1.call-update) | async-done | bytes 1703952 | tf_op jit(solution)/shard_map/psum | solution.py:143
  148.2 55.0 %all-reduce.4.cloned.1.call-done = f32[2,128,128]{2,1,0:T(8,128)} async-done(((f32[2,128,128]{2,1,0:T(8,128)}), f32[2,128,128]{2,1,0:T(8,128)}) %all-reduce.4.cloned.1.call-update) | async-done | bytes 131088 | tf_op jit(solution)/shard_map/psum | solution.py:144
  203.2 2.7 %copy.25 = f32[24,4,4096]{2,1,0:T(4,128)} copy(f32[24,4,4096]{2,1,0:T(4,128)} %get-tuple-element.33) | data formatting | bytes 3145728
  205.9 0.7 copy.26
  (93 shorter events, 18.3 us)
Async XLA Ops:
  7.2 7.5 %copy-start = (bf16[24,4,4096]{2,1,0:T(4,128)(2,1)S(1)}, bf16[24,4,4096]{2,1,0:T(4,128)(2,1)}, u32[]{:S(2)}) copy-start(bf16[24,4,4096]{2,1,0:T(4,128)(2,1)} %param.5) | copy-start | bytes 2359300
  7.2 4.6 %copy-start.1 = (s32[32,6]{0,1:T(8,128)S(1)}, s32[32,6]{0,1:T(8,128)}, u32[]{:S(2)}) copy-start(s32[32,6]{0,1:T(8,128)} %param.6) | copy-start | bytes 2308
  17.2 17.8 %all-to-all-start = ((bf16[8,3,4,4096]{3,2,1,0:T(4,128)(2,1)}), bf16[8,3,4,4096]{3,2,1,0:T(4,128)(2,1)S(1)}, u32[]{:S(2)}, u32[]{:S(2)}) async-start(bf16[8,3,4,4096]{3,2,1,0:T(4,128)(2,1)} %broadcast_select_fusion), calls=%async_computation | async-start | bytes 1572864 | tf_op jit(solution)/shard_map/all_to_all | solution.py:97
  36.2 1.1 copy-start.2
  38.7 4.1 %copy-start.4 = (f32[1,128,128]{2,1,0:T(8,128)S(1)}, f32[1,128,128]{2,1,0:T(8,128)}, u32[]{:S(2)}) copy-start(f32[1,128,128]{2,1,0:T(8,128)} %param.9) | copy-start | bytes 196612
  55.9 16.1 %all-to-all-start.1 = ((bf16[8,3,4,4096]{3,2,1,0:T(4,128)(2,1)}), bf16[8,3,4,4096]{3,2,1,0:T(4,128)(2,1)S(1)}, u32[]{:S(2)}, u32[]{:S(2)}) async-start(bf16[8,3,4,4096]{3,2,1,0:T(4,128)(2,1)} %bitcast.23), calls=%async_computation.1 | async-start | bytes 1572864 | tf_op jit(solution)/shard_map/all_to_all | solution.py:132
  59.4 88.7 %all-reduce.6.cloned.1.call-start = ((), (), s32[]{:S(2)}) async-start(), calls=%async_computation.3 | async-start | bytes 3407872 | tf_op jit(solution)/shard_map/psum | solution.py:143
  75.0 128.2 %all-reduce.4.cloned.1.call-start = ((), (), s32[]{:S(2)}) async-start(), calls=%async_computation.2 | async-start | bytes 262144 | tf_op jit(solution)/shard_map/psum | solution.py:144
  203.2 2.7 %copy-start.3 = (f32[2,128,128]{2,1,0:T(8,128)S(1)}, f32[2,128,128]{2,1,0:T(8,128)}, u32[]{:S(2)}) copy-start(f32[2,128,128]{2,1,0:T(8,128)} %all-reduce.4.cloned.1.call-done) | copy-start | bytes 393220
Sparse Core Ops, SparseCore 0:
  75.1 73.0 all-reduce.5
  151.2 51.9 all-reduce.3
where the time goes:
time: 214 us; the launch traced here: 213 us
  waiting for transfers between devices  145 us (68%)
  local copies, waits for them, and re-layouts  22.1 us (10%)
  between operations  19.8 us (9%)
  matrix products  15.1 us (7%)
  starting transfers between devices  8.8 us (4%)
  other arithmetic  2.96 us (1%)
    psum x1, waiting for transfers between devices, per_device(): tile_total, probe_layer = lax.psum((local_sum, probe_part), 'tile')  73.1 us
    psum x1, waiting for transfers between devices, per_device(): probe_total = lax.psum(probe_layer, 'pos')  55 us
    dot_general x40, matrix products, matmul_hi(): jnp.dot(left_op, right_op, precision=lax.Precision.HIGHEST, preferred_ele...  14.7 us
    all_to_all x1, waiting for transfers between devices, per_device(): lax.all_to_all(outgoing, 'pos', split_axis=0, concat_axis=0, tiled=True)  11.6 us
    all_to_all x1, starting transfers between devices, per_device(): lax.all_to_all(chosen, 'pos', split_axis=0, concat_axis=0, tiled=True)  5.17 us
    all_to_all x1, waiting for transfers between devices, per_device(): lax.all_to_all(chosen, 'pos', split_axis=0, concat_axis=0, tiled=True)  4.98 us
  transfers between devices with their start and end apart: 4, of which 4 were waited for; matrix products, arithmetic and copies ran while one was open for 3% of the time, Pallas kernels for 0%

commit v1 on v0

--- a/solution.py
+++ b/solution.py
@@ -1,8 +1,12 @@
+import functools
 import math
 
 import jax
 import jax.numpy as jnp
+import numpy as np
 from jax import lax
+from jax.experimental import pallas as pl
+from jax.experimental.pallas import tpu as pltpu
 from jax.sharding import PartitionSpec as P
 
 TS = 64
@@ -49,7 +53,16 @@
     return (left_re * right_re - left_im * right_im, left_re * right_im + left_im * right_re)
 
 
-def per_device(obj_tiles, tile_map, offsets, probe, intens):
+def pick(table, ids):
+    rows = jnp.arange(table.shape[0], dtype=jnp.int32)
+    chooser = (ids.reshape(-1)[:, None] == rows[None, :]).astype(table.dtype)
+    flat = jnp.dot(
+        chooser, table.reshape(table.shape[0], -1), preferred_element_type=jnp.float32
+    ).astype(table.dtype)
+    return flat.reshape(ids.shape + table.shape[1:])
+
+
+def general_plan(obj_tiles, tile_map, offsets, probe, intens):
     owners = lax.axis_size("pos")
     layers = lax.axis_size("tile")
     me_pos = lax.axis_index("pos")
@@ -81,7 +94,7 @@
     send_local = jnp.sum(jnp.where(matches, peer_local[:, :, None], 0), axis=1)
     send_live = jnp.any(matches, axis=1)
     chosen = jnp.where(
-        send_live[:, :, None, None], obj_tiles[send_local], jnp.zeros((), obj_tiles.dtype)
+        send_live[:, :, None, None], pick(obj_tiles, send_local), jnp.zeros((), obj_tiles.dtype)
     )
     my_corner = lax.dynamic_index_in_dim(offsets, me_pos * layers + me_tile, 0, keepdims=False)
     my_owner, my_local = footprint(my_corner)
@@ -96,7 +109,9 @@
     probe_im = probe[1]
     received = lax.all_to_all(chosen, "pos", split_axis=0, concat_axis=0, tiled=True)
     n_comps = received.shape[2]
-    pieces = received.reshape(owners * slots, n_comps, tile_edge * tile_edge)[flat_slot]
+    pieces = pick(
+        received.reshape(owners * slots, n_comps, tile_edge * tile_edge), flat_slot
+    )
     region = pieces.reshape(tile_span, tile_span, n_comps, tile_edge, tile_edge).transpose(
         2, 0, 3, 1, 4
     )
@@ -145,9 +160,370 @@
     return (tile_total.reshape(tiles_dev, 4, tile_edge * tile_edge), probe_total)
 
 
+MESH = pl.DeviceIdType.MESH
+VM = pltpu.VMEM
+SM = pltpu.SMEM
+
+
+def one_hot(rows, cols, shift):
+    row = lax.broadcasted_iota(jnp.int32, (rows, cols), 0)
+    col = lax.broadcasted_iota(jnp.int32, (rows, cols), 1)
+    return jnp.where(col == row + shift, 1.0, 0.0).astype(jnp.bfloat16)
+
+
+def bdot(a, b):
+    return jnp.dot(a, b, preferred_element_type=jnp.float32)
+
+
+def class_of(tmap, me, per):
+    found = jnp.int32(0)
+    for r in range(OWN_R):
+        found = jnp.where(lax.div(tmap[r, 0], per) == me, r, found)
+    return found
+
+
+def place(off, n, rho):
+    y = off[n, 0]
+    x = off[n, 1]
+    ty = lax.div(y, TS)
+    tx = lax.div(x, TS)
+    step = lax.rem(rho - ty + 64 * OWN_R, OWN_R)
+    return ty + step, tx, x - tx * TS, step < 3
+
+
+def pack_kernel(owners, layers, per, off, tmap, tiles, slots):
+    me = lax.axis_index("pos")
+    z = lax.axis_index("tile")
+    rho = class_of(tmap, me, per)
+    for p in range(owners):
+        row, tx, ix, live = place(off, p * layers + z, rho)
+
+        @pl.when(live)
+        def _():
+            acc = None
+            for j in range(3):
+                local = tmap[row, tx + j] - me * per
+                part = bdot(tiles[local], one_hot(TS, 2 * TS, TS * j - ix))
+                acc = part if acc is None else acc + part
+            slots[p] = acc.astype(jnp.bfloat16)
+
+
+def fetch_kernel(owners, slots, got, send_sem, recv_sem, own_sem):
+    me = lax.axis_index("pos")
+    z = lax.axis_index("tile")
+    barrier = pltpu.get_barrier_semaphore()
+    for d in range(1, owners):
+        peer = lax.rem(me + d, owners)
+        pl.semaphore_signal(barrier, inc=1, device_id=(peer, z), device_id_type=MESH)
+    own = pltpu.make_async_copy(slots.at[me], got.at[me], own_sem)
+    own.start()
+    pl.semaphore_wait(barrier, owners - 1)
+    copies = []
+    for d in range(1, owners):
+        peer = lax.rem(me + d, owners)
+        copy = pltpu.make_async_remote_copy(
+            src_ref=slots.at[peer],
+            dst_ref=got.at[me],
+            send_sem=send_sem.at[d],
+            recv_sem=recv_sem.at[d],
+            device_id=(peer, z),
+            device_id_type=MESH,
+        )
+        copy.start()
+        copies.append(copy)
+    own.wait()
+    for copy in copies:
+        copy.wait()
+
+
+def split(a):
+    high = a.astype(jnp.bfloat16)
+    return high, (a - high.astype(jnp.float32)).astype(jnp.bfloat16)
+
+
+def rmul(a, table):
+    high, low = split(a)
+    return bdot(high, table[0]) + (bdot(low, table[0]) + bdot(high, table[1]))
+
+
+def lmul(table, a):
+    high, low = split(a)
+    return bdot(table[0], high) + (bdot(table[0], low) + bdot(table[1], high))
+
+
+def both_sides(re, im, right, left):
+    width = re.shape[1]
+    mid = rmul(jnp.concatenate([re, im], axis=1), right)
+    out = lmul(left, jnp.concatenate([mid[:, :width], mid[:, width:]], axis=0))
+    return out[:width], out[width:]
+
+
+def wave_kernel(layers, per, off, tmap, got, probe, intens, tables, slots, pgrad):
+    n = lax.axis_index("pos") * layers + lax.axis_index("tile")
+    y = off[n, 0]
+    ty = lax.div(y, TS)
+    iy = y - ty * TS
+    w = probe.shape[-1]
+    owner = [lax.div(tmap[ty + s, 0], per) for s in range(3)]
+    rows = []
+    for s in range(3):
+        block = got[owner[s]]
+        rows.append(jnp.concatenate([block[k * TS : (k + 1) * TS] for k in range(4)], axis=1))
+    patch = bdot(one_hot(w, 3 * TS, iy), jnp.concatenate(rows, axis=0))
+    en_re, en_im, ex_re, ex_im = (patch[:, k * w : (k + 1) * w] for k in range(4))
+    pr, pi = probe[0], probe[1]
+    fw, fc, aw, ac = ((tables[2 * i], tables[2 * i + 1]) for i in range(4))
+    re, im = product(pr, pi, en_re, en_im)
+    sp_re, sp_im = both_sides(re, im, aw, ac)
+    re, im = product(sp_re, sp_im, ex_re, ex_im)
+    far_re, far_im = both_sides(re, im, fw, fc)
+    excess = far_re * far_re + far_im * far_im - intens[0]
+    bk_re, bk_im = both_sides(excess * far_re, excess * far_im, fc, fw)
+    gx_re, gx_im = product(sp_re, -sp_im, bk_re, bk_im)
+    re, im = product(ex_re, -ex_im, bk_re, bk_im)
+    in_re, in_im = both_sides(re, im, ac, aw)
+    ge_re, ge_im = product(pr, -pi, in_re, in_im)
+    gp_re, gp_im = product(en_re, -en_im, in_re, in_im)
+    pgrad[0:w] = gp_re
+    pgrad[w : 2 * w] = gp_im
+    grad = jnp.concatenate([ge_re, ge_im, gx_re, gx_im], axis=1).astype(jnp.bfloat16)
+    region = bdot(one_hot(3 * TS, w, -iy), grad).astype(jnp.bfloat16)
+    for s in range(3):
+        for k in range(4):
+            slots[owner[s], k * TS : (k + 1) * TS, :] = region[
+                s * TS : (s + 1) * TS, k * w : (k + 1) * w
+            ]
+
+
+def spread_kernel(
+    owners, layers, slots, pgrad, got, ptotal, part, summed, layer_part,
+    own_sem, a_send, a_recv, up_send, up_recv, dn_send, dn_recv,
+    p_send, p_recv, q_send, q_recv, r_send, r_recv,
+):
+    me = lax.axis_index("pos")
+    z = lax.axis_index("tile")
+    chunk = pgrad.shape[0] // owners
+
+    def remote(src, dst, ssem, rsem, p, t):
+        return pltpu.make_async_remote_copy(
+            src_ref=src, dst_ref=dst, send_sem=ssem, recv_sem=rsem,
+            device_id=(p, t), device_id_type=MESH,
+        )
+
+    barrier = pltpu.get_barrier_semaphore()
+    for d in range(1, owners):
+        pl.semaphore_signal(
+            barrier, inc=1, device_id=(lax.rem(me + d, owners), z), device_id_type=MESH
+        )
+    for d in range(1, layers):
+        pl.semaphore_signal(
+            barrier, inc=1, device_id=(me, lax.rem(z + d, layers)), device_id_type=MESH
+        )
+    own = pltpu.make_async_copy(slots.at[me], got.at[z, me], own_sem)
+    own.start()
+    pl.semaphore_wait(barrier, owners + layers - 2)
+
+    probes, shares = [], []
+    for d in range(1, owners):
+        peer = lax.rem(me + d, owners)
+        probes.append(
+            remote(
+                pgrad.at[pl.ds(pl.multiple_of(peer * chunk, chunk), chunk)],
+                part.at[me], p_send.at[d], p_recv.at[d], peer, z,
+            )
+        )
+        probes[-1].start()
+    for d in range(1, owners):
+        peer = lax.rem(me + d, owners)
+        shares.append(remote(slots.at[peer], got.at[z, me], a_send.at[d], a_recv.at[d], peer, z))
+        shares[-1].start()
+
+    def up(t, p, item, target):
+        ref = got.at[item, p]
+        return remote(ref, ref, up_send.at[t, p], up_recv.at[t, p], me, target)
+
+    def down(t, p, item, target):
+        ref = got.at[item, p]
+        return remote(ref, ref, dn_send.at[t, p], dn_recv.at[t, p], me, target)
+
+    def first(p):
+        @pl.when(z < layers - 1)
+        def _():
+            up(0, p, z, z + 1).start()
+
+        @pl.when(z > 0)
+        def _():
+            down(0, p, z, z - 1).start()
+
+    own.wait()
+    first(me)
+    part[me] = pgrad[pl.ds(pl.multiple_of(me * chunk, chunk), chunk)]
+    for copy in probes:
+        copy.wait()
+    summed[...] = jnp.sum(part[...], axis=0)
+    layer_part[z] = summed[...]
+    zs = []
+    for d in range(1, layers):
+        zs.append(
+            remote(
+                summed, layer_part.at[z], q_send.at[d], q_recv.at[d],
+                me, lax.rem(z + d, layers),
+            )
+        )
+        zs[-1].start()
+    for d in range(1, owners):
+        shares[d - 1].wait_recv()
+        first(lax.rem(me - d + owners, owners))
+    for copy in zs:
+        copy.wait()
+    ptotal[me] = jnp.sum(layer_part[...], axis=0)
+    outs = []
+    for d in range(1, owners):
+        outs.append(
+            remote(
+                ptotal.at[me], ptotal.at[me], r_send.at[d], r_recv.at[d],
+                lax.rem(me + d, owners), z,
+            )
+        )
+        outs[-1].start()
+
+    for t in range(layers - 1):
+        @pl.loop(0, owners)
+        def _(i):
+            p = lax.rem(me - i + owners, owners)
+
+            @pl.when(z - 1 - t >= 0)
+            def _():
+                up(t, p, z - 1 - t, z - 1).wait_recv()
+                if t < layers - 2:
+
+                    @pl.when(z < layers - 1)
+                    def _():
+                        up(t + 1, p, z - 1 - t, z + 1).start()
+
+            @pl.when(z + 1 + t <= layers - 1)
+            def _():
+                down(t, p, z + 1 + t, z + 1).wait_recv()
+                if t < layers - 2:
+
+                    @pl.when(z > 0)
+                    def _():
+                        down(t + 1, p, z + 1 + t, z - 1).start()
+
+    for copy in shares:
+        copy.wait_send()
+    for copy in outs:
+        copy.wait()
+    for t in range(layers - 1):
+        @pl.loop(0, owners)
+        def _(p):
+            @pl.when((z - t >= 0) & (z < layers - 1))
+            def _():
+                up(t, p, z - t, z + 1).wait_send()
+
+            @pl.when((z + t <= layers - 1) & (z > 0))
+            def _():
+                down(t, p, z + t, z - 1).wait_send()
+
+
+def add_kernel(owners, layers, per, off, tmap, got, out):
+    me = lax.axis_index("pos")
+    rho = class_of(tmap, me, per)
+    out[...] = jnp.zeros_like(out)
+
+    @pl.loop(0, owners * layers)
+    def _(n):
+        row, tx, ix, live = place(off, n, rho)
+
+        @pl.when(live)
+        def _():
+            block = got[lax.rem(n, layers), lax.div(n, layers)]
+            for j in range(3):
+                local = tmap[row, tx + j] - me * per
+                out[local] += bdot(block, one_hot(2 * TS, TS, ix - TS * j))
+
+
+def spectral_blocks(width):
+    k = np.arange(width)
+    fwd = np.exp(-2j * np.pi * (np.outer(k, k) % width) / width) / np.sqrt(width)
+    centred = (k + width // 2) % width - width // 2
+    phase = np.exp(-0.2j * centred * centred / width)
+    ahead = np.conj(fwd) @ (phase[:, None] * fwd)
+    found = []
+    for m in (fwd, np.conj(fwd), ahead, np.conj(ahead)):
+        full = np.block([[m.real, m.imag], [-m.imag, m.real]]).astype(np.float32)
+        high = full.astype(jnp.bfloat16)
+        found += [high, (full - high.astype(np.float32)).astype(jnp.bfloat16)]
+    return np.stack(found)
+
+
+def params(**kw):
+    return pltpu.CompilerParams(vmem_limit_bytes=32 * 1024 * 1024, **kw)
+
+
+def row_plan(obj_tiles, tile_map, offsets, probe, intens):
+    owners = lax.axis_size("pos")
+    layers = lax.axis_size("tile")
+    per = obj_tiles.shape[0]
+    w = probe.shape[-1]
+    bf, f32 = jnp.bfloat16, jnp.float32
+    vm = pl.BlockSpec(memory_space=VM)
+    sm = pl.BlockSpec(memory_space=SM)
+    dma = pltpu.SemaphoreType.DMA
+    tiles = obj_tiles.reshape(per, 4 * TS, TS)
+    slot_shape = jax.ShapeDtypeStruct((owners, 4 * TS, w), bf)
+    slots = pl.pallas_call(
+        functools.partial(pack_kernel, owners, layers, per),
+        out_shape=slot_shape,
+        in_specs=[sm, sm, vm],
+        out_specs=vm,
+        compiler_params=params(),
+    )(offsets, tile_map, tiles)
+    got = pl.pallas_call(
+        functools.partial(fetch_kernel, owners),
+        out_shape=slot_shape,
+        in_specs=[vm],
+        out_specs=vm,
+        scratch_shapes=[dma((owners,)), dma((owners,)), dma],
+        compiler_params=params(collective_id=0, has_side_effects=True),
+    )(slots)
+    tables = jnp.asarray(spectral_blocks(w))
+    grads, pgrad = pl.pallas_call(
+        functools.partial(wave_kernel, layers, per),
+        out_shape=[slot_shape, jax.ShapeDtypeStruct((2 * w, w), f32)],
+        in_specs=[sm, sm, vm, vm, vm, vm],
+        out_specs=[vm, vm],
+        compiler_params=params(),
+    )(offsets, tile_map, got, probe, intens, tables)
+    chunk = 2 * w // owners
+    spread, ptotal = pl.pallas_call(
+        functools.partial(spread_kernel, owners, layers),
+        out_shape=[
+            jax.ShapeDtypeStruct((layers, owners, 4 * TS, w), bf),
+            jax.ShapeDtypeStruct((owners, chunk, w), f32),
+        ],
+        in_specs=[vm, vm],
+        out_specs=[vm, vm],
+        scratch_shapes=[
+            VM((owners, chunk, w), f32), VM((chunk, w), f32), VM((layers, chunk, w), f32), dma,
+            dma((owners,)), dma((owners,)),
+            dma((layers, owners)), dma((layers, owners)), dma((layers, owners)), dma((layers, owners)),
+            dma((owners,)), dma((owners,)), dma((layers,)), dma((layers,)), dma((owners,)), dma((owners,)),
+        ],
+        compiler_params=params(collective_id=1, has_side_effects=True),
+    )(grads, pgrad)
+    total = pl.pallas_call(
+        functools.partial(add_kernel, owners, layers, per),
+        out_shape=jax.ShapeDtypeStruct((per, 4 * TS, TS), f32),
+        in_specs=[sm, sm, vm],
+        out_specs=vm,
+        compiler_params=params(),
+    )(offsets, tile_map, spread)
+    return (total.reshape(per, 4, TS * TS), ptotal.reshape(2, w, w))
+
+
 def solution(mesh):
     in_specs = (P("pos", None, None), P(), P(), P(), P(("pos", "tile"), None, None))
     out_specs = (P("pos", None, None), P())
-    return jax.shard_map(
-        per_device, mesh=mesh, in_specs=in_specs, out_specs=out_specs, check_vma=False
-    )
+    plan = row_plan if mesh.shape["pos"] == OWN_R else general_plan
+    return jax.shard_map(plan, mesh=mesh, in_specs=in_specs, out_specs=out_specs, check_vma=False)

time: 214 us -> 73.4 us (0.34)
  waiting for transfers between devices: 145 us -> 0 us
  Pallas kernels: 0 us -> 66 us
  between operations: 19.8 us -> 0.73 us
  matrix products: 15.1 us -> 0 us
  local copies, waits for them, and re-layouts: 22.1 us -> 7.07 us
  starting transfers between devices: 8.8 us -> 0 us
  other arithmetic: 2.96 us -> 0 us
    psum x2 -> x0, waiting for transfers between devices: 128 us -> none  [the longest x1 73.1 us: per_device(): tile_total, probe_layer = lax.psum((local_sum, probe_part), 'tile')]
    pallas_call x0 -> x5, Pallas kernels: none -> 66 us  [the longest x1 45.9 us: row_plan(): pl.pallas_call(functools.partial(spread_kernel, owners, layers), out_shap...]
    all_to_all x2 -> x0, waiting for transfers between devices: 16.5 us -> none  [the longest x1 11.6 us: per_device(): lax.all_to_all(outgoing, 'pos', split_axis=0, concat_axis=0, tiled=True)]
    dot_general x41 -> x0, matrix products: 15.1 us -> none  [the longest x40 14.7 us: matmul_hi(): jnp.dot(left_op, right_op, precision=lax.Precision.HIGHEST, preferred_ele...]
    all_to_all x2 -> x0, starting transfers between devices: 8.72 us -> none  [the longest x1 5.17 us: per_device(): lax.all_to_all(chosen, 'pos', split_axis=0, concat_axis=0, tiled=True)]
    gather x4 -> x0, local copies, waits for them, and re-layouts: 3.99 us -> none  [the longest x2 1.98 us: footprint(): store_id = tile_map[row_ids[:, None], col_ids[None, :]].reshape(-1)]
    dynamic_update_slice x1 -> x0, local copies, waits for them, and re-layouts: 2.9 us -> none  [per_device(): lax.dynamic_update_slice(region, patch_grad, (zero_idx, inner_y, inner_x))]
    scatter x1 -> x0, local copies, waits for them, and re-layouts: 2.42 us -> none  [per_device(): outgoing = jnp.zeros((owners * slots, 4, tile_edge * tile_edge), jnp.bflo...]
  transfers between devices with their start and end apart: 4 -> 0, of which waited for: 4 -> 0; matrix products, arithmetic and copies ran while one was open for 3% -> 0% of each run, Pallas kernels for 0% -> 0%
where the time goes in v1:
time: 73.4 us; the launch traced here: 73.8 us
  Pallas kernels  66 us (90%)
  local copies, waits for them, and re-layouts  7.07 us (10%)
    pallas_call x1, Pallas kernels, row_plan(): pl.pallas_call(functools.partial(spread_kernel, owners, layers), out_shap...  45.9 us
    pallas_call x1, Pallas kernels, row_plan(): pl.pallas_call(functools.partial(fetch_kernel, owners), out_shape=slot_sh...  10.4 us
    pallas_call x1, Pallas kernels, row_plan(): pl.pallas_call(functools.partial(add_kernel, owners, layers, per), out_sh...  4.59 us
    pallas_call x1, Pallas kernels, row_plan(): pl.pallas_call(functools.partial(wave_kernel, layers, per), out_shape=[sl...  3.29 us
    reshape x1, local copies, waits for them, and re-layouts, row_plan(): tiles = obj_tiles.reshape(per, 4 * TS, TS)  2.67 us
    unnamed x9, local copies, waits for them, and re-layouts  2.2 us
    reshape x1, local copies, waits for them, and re-layouts, row_plan(): return (total.reshape(per, 4, TS * TS), ptotal.reshape(2, w, w))  2.2 us
    pallas_call x1, Pallas kernels, row_plan(): pl.pallas_call(functools.partial(pack_kernel, owners, layers, per), out_s...  1.77 us

profile of v1, /device:TPU:0, one launch (start us, length us, event | category | flops | bytes accessed | tf_op | source)
XLA Modules:
  0.0 73.8 jit_solution(9951646780823229100)
XLA Ops:
  0.6 0.8 %copy.19.tmap = s32[32,6]{1,0:T(8,128)S(1)} copy(s32[32,6]{0,1:T(8,128)} %param.7) | data formatting | bytes 1536 | tf_op args[1]
  1.4 0.8 %copy.18.off = s32[32,2]{1,0:T(8,128)S(1)} copy(s32[32,2]{0,1:T(2,128)} %param.8) | data formatting | bytes 512 | tf_op args[2]
  2.2 2.7 %reshape.13.tiles = bf16[24,256,64]{2,1,0:T(8,128)(2,1)S(1)} reshape(bf16[24,4,4096]{2,1,0:T(4,128)(2,1)} %param.6) | data formatting | bytes 1572864 | tf_op jit(solution)/shard_map/reshape | solution.py:473
  4.8 0.0 copy-start
  4.8 0.0 copy-start.1
  4.9 0.0 copy-start.2
  4.9 1.8 %shard_map.77.slots = bf16[8,256,128]{2,1,0:T(8,128)(2,1)S(1)} custom-call(s32[32,2]{1,0:T(8,128)S(1)} %copy.18.off, s32[32,6]{1,0:T(8,128)S(1)} %copy.19.tmap, bf16[24,256,64]{2,1,0:T(8,128)(2,1)S(1)} %reshape.13.tiles), custom_call_target="tpu_custom_call" | custom-call | tf_op jit(solution)/shard_map/pallas_call | solution.py:475
  6.7 10.4 %shard_map.78.got = bf16[8,256,128]{2,1,0:T(8,128)(2,1)S(1)} custom-call(bf16[8,256,128]{2,1,0:T(8,128)(2,1)S(1)} %shard_map.77.slots), custom_call_target="tpu_custom_call" | custom-call | tf_op jit(solution)/shard_map/pallas_call | solution.py:482
  17.1 0.0 copy-done
  17.1 0.0 copy-done.1
  17.1 0.0 copy-done.2
  17.1 3.3 %shard_map.79 = (bf16[8,256,128]{2,1,0:T(8,128)(2,1)S(1)}, f32[256,128]{1,0:T(8,128)S(1)}) custom-call(s32[32,2]{1,0:T(8,128)S(1)} %copy.18.off, s32[32,6]{1,0:T(8,128)S(1)} %copy.19.tmap, bf16[8,256,128]{2,1,0:T(8,128)(2,1)S(1)} %shard_map.78.got, f32[2,128,128]{2,1,0:T(8,128)S(1)} %copy-done.1, f32[1,128,128]{2,1,0:T(8,128)S(1)} %copy-done.2, ...), custom_call_target="tpu_custom_call" | custom-call | tf_op jit(solution)/shard_map/pallas_call | solution.py:491
  20.4 45.9 %shard_map.80 = (bf16[4,8,256,128]{3,2,1,0:T(8,128)(2,1)S(1)}, f32[8,32,128]{2,1,0:T(8,128)S(1)}) custom-call(bf16[8,256,128]{2,1,0:T(8,128)(2,1)S(1)} %get-tuple-element.6.slots, f32[256,128]{1,0:T(8,128)S(1)} %get-tuple-element.7.pgrad), custom_call_target="tpu_custom_call" | custom-call | tf_op jit(solution)/shard_map/pallas_call | solution.py:499
  66.3 4.6 %shard_map.81 = f32[24,256,64]{2,1,0:T(8,128)S(1)} custom-call(s32[32,2]{1,0:T(8,128)S(1)} %copy.18.off, s32[32,6]{1,0:T(8,128)S(1)} %copy.19.tmap, bf16[4,8,256,128]{3,2,1,0:T(8,128)(2,1)S(1)} %get-tuple-element.8.got), custom_call_target="tpu_custom_call" | custom-call | tf_op jit(solution)/shard_map/pallas_call | solution.py:515
  70.9 2.2 %reshape.14 = f32[24,4,4096]{2,1,0:T(4,128)} reshape(f32[24,256,64]{2,1,0:T(8,128)S(1)} %shard_map.81) | data formatting | bytes 3145728 | tf_op jit(solution)/shard_map/reshape | solution.py:522
  73.1 0.7 copy.21
Async XLA Ops:
  4.8 12.2 %copy-start = (bf16[8,256,256]{2,1,0:T(8,128)(2,1)S(1)}, bf16[8,256,256]{2,1,0:T(8,128)(2,1)}, u32[]{:S(2)}) copy-start(bf16[8,256,256]{2,1,0:T(8,128)(2,1)} %constant.2.clone.tables) | copy-start | bytes 3145732
  4.8 12.2 %copy-start.1 = (f32[2,128,128]{2,1,0:T(8,128)S(1)}, f32[2,128,128]{2,1,0:T(8,128)}, u32[]{:S(2)}) copy-start(f32[2,128,128]{2,1,0:T(8,128)} %probe.1) | copy-start | bytes 393220
  4.9 12.2 %copy-start.2 = (f32[1,128,128]{2,1,0:T(8,128)S(1)}, f32[1,128,128]{2,1,0:T(8,128)}, u32[]{:S(2)}) copy-start(f32[1,128,128]{2,1,0:T(8,128)} %intens.1) | copy-start | bytes 196612

commit v2 on v1

--- a/solution.py
+++ b/solution.py
@@ -258,7 +258,7 @@
     return out[:width], out[width:]
 
 
-def wave_kernel(layers, per, off, tmap, got, probe, intens, tables, slots, pgrad):
+def wave_kernel(layers, per, off, tmap, got, probe, intens, tables, patch_out, pgrad):
     n = lax.axis_index("pos") * layers + lax.axis_index("tile")
     y = off[n, 0]
     ty = lax.div(y, TS)
@@ -286,23 +286,25 @@
     gp_re, gp_im = product(en_re, -en_im, in_re, in_im)
     pgrad[0:w] = gp_re
     pgrad[w : 2 * w] = gp_im
-    grad = jnp.concatenate([ge_re, ge_im, gx_re, gx_im], axis=1).astype(jnp.bfloat16)
-    region = bdot(one_hot(3 * TS, w, -iy), grad).astype(jnp.bfloat16)
-    for s in range(3):
-        for k in range(4):
-            slots[owner[s], k * TS : (k + 1) * TS, :] = region[
-                s * TS : (s + 1) * TS, k * w : (k + 1) * w
-            ]
+    for k, part in enumerate((ge_re, ge_im, gx_re, gx_im)):
+        patch_out[k // 2, (k % 2) * w : (k % 2 + 1) * w, :] = part.astype(jnp.bfloat16)
 
 
 def spread_kernel(
-    owners, layers, slots, pgrad, got, ptotal, part, summed, layer_part,
-    own_sem, a_send, a_recv, up_send, up_recv, dn_send, dn_recv,
+    owners, layers, patch, pgrad, got, ptotal, part, summed, layer_part,
+    own_sem, l_send, l_recv, z_send, z_recv, c_send, c_recv,
     p_send, p_recv, q_send, q_recv, r_send, r_recv,
 ):
     me = lax.axis_index("pos")
     z = lax.axis_index("tile")
+    core = lax.rem(me, 2)
+    x = lax.rem(lax.div(me, 2), 2)
+    y = lax.div(me, 4)
+    mates = [4 * b + 2 * a for b in (y, 1 - y) for a in (x, 1 - x)]
+    same = [m + core for m in mates]
+    other = [m + 1 - core for m in mates]
     chunk = pgrad.shape[0] // owners
+    half = patch.shape[1] // 2
 
     def remote(src, dst, ssem, rsem, p, t):
         return pltpu.make_async_remote_copy(
@@ -319,11 +321,57 @@
         pl.semaphore_signal(
             barrier, inc=1, device_id=(me, lax.rem(z + d, layers)), device_id_type=MESH
         )
-    own = pltpu.make_async_copy(slots.at[me], got.at[z, me], own_sem)
+    own = pltpu.make_async_copy(patch, got.at[:, z, me], own_sem)
     own.start()
     pl.semaphore_wait(barrier, owners + layers - 2)
 
-    probes, shares = [], []
+    def item(h, t, p, rows=None):
+        ref = got.at[h, t, p]
+        return ref if rows is None else ref.at[pl.ds(rows * half, half)]
+
+    def across(h, t, i):
+        return remote(
+            item(h, t, me), item(h, t, me), l_send.at[h, t, i], l_recv.at[h, t, i], same[i], z
+        )
+
+    def arrived(h, t, i):
+        return remote(
+            item(h, t, same[i]), item(h, t, same[i]),
+            l_send.at[h, t, i], l_recv.at[h, t, i], same[i], z,
+        )
+
+    def corner(h, t, r, came, to):
+        ref = item(h, t, same[came], r)
+        k = 0 if r == 0 else 3
+        return remote(ref, ref, l_send.at[h, t, k], l_recv.at[h, t, k], same[to], z)
+
+    def corner_in(h, t, r):
+        ref = item(h, t, same[3], r)
+        k = 0 if r == 0 else 3
+        return remote(ref, ref, l_send.at[h, t, k], l_recv.at[h, t, k], same[3], z)
+
+    def hand(h, t, i):
+        ref = item(h, t, same[i])
+        return remote(ref, ref, c_send.at[h, t, i], c_recv.at[h, t, i], other[0], z)
+
+    def handed(h, t, i):
+        ref = item(h, t, other[i])
+        return remote(ref, ref, c_send.at[h, t, i], c_recv.at[h, t, i], other[0], z)
+
+    def climb(h, way, t, i, layer, target):
+        ref = item(h, layer, same[i])
+        return remote(ref, ref, z_send.at[h, way, t, i], z_recv.at[h, way, t, i], me, target)
+
+    def leave(h, i):
+        @pl.when(z < layers - 1)
+        def _():
+            climb(h, 0, 0, i, z, z + 1).start()
+
+        @pl.when(z > 0)
+        def _():
+            climb(h, 1, 0, i, z, z - 1).start()
+
+    probes = []
     for d in range(1, owners):
         peer = lax.rem(me + d, owners)
         probes.append(
@@ -333,30 +381,16 @@
             )
         )
         probes[-1].start()
-    for d in range(1, owners):
-        peer = lax.rem(me + d, owners)
-        shares.append(remote(slots.at[peer], got.at[z, me], a_send.at[d], a_recv.at[d], peer, z))
-        shares[-1].start()
-
-    def up(t, p, item, target):
-        ref = got.at[item, p]
-        return remote(ref, ref, up_send.at[t, p], up_recv.at[t, p], me, target)
-
-    def down(t, p, item, target):
-        ref = got.at[item, p]
-        return remote(ref, ref, dn_send.at[t, p], dn_recv.at[t, p], me, target)
-
-    def first(p):
-        @pl.when(z < layers - 1)
-        def _():
-            up(0, p, z, z + 1).start()
-
-        @pl.when(z > 0)
-        def _():
-            down(0, p, z, z - 1).start()
-
     own.wait()
-    first(me)
+    across(0, z, 1).start()
+    across(0, z, 2).start()
+    leave(1, 0)
+    leave(0, 0)
+    across(1, z, 1).start()
+    across(1, z, 2).start()
+    hand(0, z, 0).start()
+    hand(1, z, 0).start()
+
     part[me] = pgrad[pl.ds(pl.multiple_of(me * chunk, chunk), chunk)]
     for copy in probes:
         copy.wait()
@@ -371,9 +405,45 @@
             )
         )
         zs[-1].start()
-    for d in range(1, owners):
-        shares[d - 1].wait_recv()
-        first(lax.rem(me - d + owners, owners))
+
+    def sides(h, t):
+        arrived(h, t, 1).wait_recv()
+        corner(h, t, 0, 1, 2).start()
+        hand(h, t, 1).start()
+        if h == 0:
+            leave(0, 1)
+        arrived(h, t, 2).wait_recv()
+        corner(h, t, 1, 2, 1).start()
+        hand(h, t, 2).start()
+        if h == 0:
+            leave(0, 2)
+
+    def last(h, t):
+        corner_in(h, t, 0).wait_recv()
+        corner_in(h, t, 1).wait_recv()
+        hand(h, t, 3).start()
+        if h == 0:
+            leave(0, 3)
+
+    def step_z(h, t, i):
+        for way, layer, there in ((0, z - 1 - t, z + 1), (1, z + 1 + t, z - 1)):
+            @pl.when((layer >= 0) & (layer <= layers - 1))
+            def _():
+                climb(h, way, t, i, layer, there).wait_recv()
+                if t < layers - 2:
+
+                    @pl.when((there >= 0) & (there <= layers - 1))
+                    def _():
+                        climb(h, way, t + 1, i, layer, there).start()
+
+                hand(h, layer, i).start()
+                if h == 1:
+                    across(1, layer, 1).start()
+                    across(1, layer, 2).start()
+
+    sides(0, z)
+    step_z(1, 0, 0)
+    last(0, z)
     for copy in zs:
         copy.wait()
     ptotal[me] = jnp.sum(layer_part[...], axis=0)
@@ -386,44 +456,51 @@
             )
         )
         outs[-1].start()
-
+    sides(1, z)
     for t in range(layers - 1):
-        @pl.loop(0, owners)
-        def _(i):
-            p = lax.rem(me - i + owners, owners)
-
-            @pl.when(z - 1 - t >= 0)
+        if t > 0:
+            step_z(1, t, 0)
+        for i in range(4):
+            step_z(0, t, i)
+        if t == 0:
+            last(1, z)
+        for layer in (z - 1 - t, z + 1 + t):
+            @pl.when((layer >= 0) & (layer <= layers - 1))
             def _():
-                up(t, p, z - 1 - t, z - 1).wait_recv()
-                if t < layers - 2:
-
-                    @pl.when(z < layers - 1)
-                    def _():
-                        up(t + 1, p, z - 1 - t, z + 1).start()
-
-            @pl.when(z + 1 + t <= layers - 1)
-            def _():
-                down(t, p, z + 1 + t, z + 1).wait_recv()
-                if t < layers - 2:
-
-                    @pl.when(z > 0)
-                    def _():
-                        down(t + 1, p, z + 1 + t, z - 1).start()
-
-    for copy in shares:
-        copy.wait_send()
+                sides(1, layer)
+                last(1, layer)
+
     for copy in outs:
         copy.wait()
+
+    @pl.loop(0, layers)
+    def _(t):
+        for h in range(2):
+            for i in range(4):
+                hand(h, t, i).wait_send()
+                handed(h, t, i).wait_recv()
+
+    def drained(h, t):
+        across(h, t, 1).wait_send()
+        across(h, t, 2).wait_send()
+        corner(h, t, 0, 1, 2).wait_send()
+        corner(h, t, 1, 2, 1).wait_send()
+
+    drained(0, z)
+
+    @pl.loop(0, layers)
+    def _(t):
+        drained(1, t)
+
     for t in range(layers - 1):
-        @pl.loop(0, owners)
-        def _(p):
-            @pl.when((z - t >= 0) & (z < layers - 1))
+        for way, layer, there in ((0, z - t, z + 1), (1, z + t, z - 1)):
+            @pl.when(
+                (layer >= 0) & (layer <= layers - 1) & (there >= 0) & (there <= layers - 1)
+            )
             def _():
-                up(t, p, z - t, z + 1).wait_send()
-
-            @pl.when((z + t <= layers - 1) & (z > 0))
-            def _():
-                down(t, p, z + t, z - 1).wait_send()
+                climb(1, way, t, 0, layer, there).wait_send()
+                for i in range(4):
+                    climb(0, way, t, i, layer, there).wait_send()
 
 
 def add_kernel(owners, layers, per, off, tmap, got, out):
@@ -437,10 +514,16 @@
 
         @pl.when(live)
         def _():
-            block = got[lax.rem(n, layers), lax.div(n, layers)]
+            w = 2 * TS
+            pick_rows = one_hot(TS, w, row * TS - off[n, 0])
+            t, p = lax.rem(n, layers), lax.div(n, layers)
+            first, second = got[0, t, p], got[1, t, p]
+            wide = jnp.concatenate([first[:w], first[w:], second[:w], second[w:]], axis=1)
+            rows = bdot(pick_rows, wide).astype(jnp.bfloat16)
+            block = jnp.concatenate([rows[:, k * w : (k + 1) * w] for k in range(4)], axis=0)
             for j in range(3):
                 local = tmap[row, tx + j] - me * per
-                out[local] += bdot(block, one_hot(2 * TS, TS, ix - TS * j))
+                out[local] += bdot(block, one_hot(w, TS, ix - TS * j))
 
 
 def spectral_blocks(width):
@@ -490,7 +573,10 @@
     tables = jnp.asarray(spectral_blocks(w))
     grads, pgrad = pl.pallas_call(
         functools.partial(wave_kernel, layers, per),
-        out_shape=[slot_shape, jax.ShapeDtypeStruct((2 * w, w), f32)],
+        out_shape=[
+            jax.ShapeDtypeStruct((2, 2 * w, w), bf),
+            jax.ShapeDtypeStruct((2 * w, w), f32),
+        ],
         in_specs=[sm, sm, vm, vm, vm, vm],
         out_specs=[vm, vm],
         compiler_params=params(),
@@ -499,15 +585,16 @@
     spread, ptotal = pl.pallas_call(
         functools.partial(spread_kernel, owners, layers),
         out_shape=[
-            jax.ShapeDtypeStruct((layers, owners, 4 * TS, w), bf),
+            jax.ShapeDtypeStruct((2, layers, owners, 2 * w, w), bf),
             jax.ShapeDtypeStruct((owners, chunk, w), f32),
         ],
         in_specs=[vm, vm],
         out_specs=[vm, vm],
         scratch_shapes=[
             VM((owners, chunk, w), f32), VM((chunk, w), f32), VM((layers, chunk, w), f32), dma,
-            dma((owners,)), dma((owners,)),
-            dma((layers, owners)), dma((layers, owners)), dma((layers, owners)), dma((layers, owners)),
+            dma((2, layers, 4)), dma((2, layers, 4)),
+            dma((2, 2, layers, 4)), dma((2, 2, layers, 4)),
+            dma((2, layers, 4)), dma((2, layers, 4)),
             dma((owners,)), dma((owners,)), dma((layers,)), dma((layers,)), dma((owners,)), dma((owners,)),
         ],
         compiler_params=params(collective_id=1, has_side_effects=True),

time: 73.4 us -> 66.9 us (0.911); the launches traced: 73.8 us -> 66.3 us
  Pallas kernels: 66 us -> 58.5 us
    pallas_call x1, Pallas kernels: 45.9 us -> 37.1 us  [row_plan(): pl.pallas_call(functools.partial(spread_kernel, owners, layers), out_shap...]
    pallas_call x1, Pallas kernels: 4.59 us -> 5.91 us  [row_plan(): pl.pallas_call(functools.partial(add_kernel, owners, layers, per), out_sh...]
where the time goes in v2:
time: 66.9 us; the launch traced here: 66.3 us
  Pallas kernels  58.5 us (87%)
  local copies, waits for them, and re-layouts  7.16 us (11%)
  between operations  0.73 us (1%)
    pallas_call x1, Pallas kernels, row_plan(): pl.pallas_call(functools.partial(spread_kernel, owners, layers), out_shap...  37.1 us
    pallas_call x1, Pallas kernels, row_plan(): pl.pallas_call(functools.partial(fetch_kernel, owners), out_shape=slot_sh...  11 us
    pallas_call x1, Pallas kernels, row_plan(): pl.pallas_call(functools.partial(add_kernel, owners, layers, per), out_sh...  5.91 us
    pallas_call x1, Pallas kernels, row_plan(): pl.pallas_call(functools.partial(wave_kernel, layers, per), out_shape=[ja...  3.12 us
    reshape x1, local copies, waits for them, and re-layouts, row_plan(): tiles = obj_tiles.reshape(per, 4 * TS, TS)  2.67 us
    unnamed x9, local copies, waits for them, and re-layouts  2.29 us
    reshape x1, local copies, waits for them, and re-layouts, row_plan(): return (total.reshape(per, 4, TS * TS), ptotal.reshape(2, w, w))  2.2 us
    pallas_call x1, Pallas kernels, row_plan(): pl.pallas_call(functools.partial(pack_kernel, owners, layers, per), out_s...  1.4 us

profile of v2, /device:TPU:0, one launch (start us, length us, event | category | flops | bytes accessed | tf_op | source)
XLA Modules:
  0.0 66.3 jit_solution(15867066936882931080)
XLA Ops:
  0.6 0.0 copy-start
  0.6 0.0 copy-start.2
  0.7 0.0 copy-start.1
  0.7 0.9 %copy.19.tmap = s32[32,6]{1,0:T(8,128)S(1)} copy(s32[32,6]{0,1:T(8,128)} %param.7) | data formatting | bytes 1536 | tf_op args[1]
  1.5 0.8 %copy.18.off = s32[32,2]{1,0:T(8,128)S(1)} copy(s32[32,2]{0,1:T(2,128)} %param.8) | data formatting | bytes 512 | tf_op args[2]
  2.3 2.7 %reshape.13.tiles = bf16[24,256,64]{2,1,0:T(8,128)(2,1)S(1)} reshape(bf16[24,4,4096]{2,1,0:T(4,128)(2,1)} %param.6) | data formatting | bytes 1572864 | tf_op jit(solution)/shard_map/reshape | solution.py:556
  5.0 1.4 %shard_map.77.slots = bf16[8,256,128]{2,1,0:T(8,128)(2,1)S(1)} custom-call(s32[32,2]{1,0:T(8,128)S(1)} %copy.18.off, s32[32,6]{1,0:T(8,128)S(1)} %copy.19.tmap, bf16[24,256,64]{2,1,0:T(8,128)(2,1)S(1)} %reshape.13.tiles), custom_call_target="tpu_custom_call" | custom-call | tf_op jit(solution)/shard_map/pallas_call | solution.py:558
  6.4 11.0 %shard_map.78.got = bf16[8,256,128]{2,1,0:T(8,128)(2,1)S(1)} custom-call(bf16[8,256,128]{2,1,0:T(8,128)(2,1)S(1)} %shard_map.77.slots), custom_call_target="tpu_custom_call" | custom-call | tf_op jit(solution)/shard_map/pallas_call | solution.py:565
  17.3 0.0 copy-done
  17.3 0.0 copy-done.2
  17.3 0.0 copy-done.1
  17.4 3.1 %shard_map.79 = (bf16[2,256,128]{2,1,0:T(8,128)(2,1)S(1)}, f32[256,128]{1,0:T(8,128)S(1)}) custom-call(s32[32,2]{1,0:T(8,128)S(1)} %copy.18.off, s32[32,6]{1,0:T(8,128)S(1)} %copy.19.tmap, bf16[8,256,128]{2,1,0:T(8,128)(2,1)S(1)} %shard_map.78.got, f32[2,128,128]{2,1,0:T(8,128)S(1)} %copy-done.1, f32[1,128,128]{2,1,0:T(8,128)S(1)} %copy-done.2, ...), custom_call_target="tpu_custom_call" | custom-call | tf_op jit(solution)/shard_map/pallas_call | solution.py:574
  20.5 37.1 %shard_map.80 = (bf16[2,4,8,256,128]{4,3,2,1,0:T(8,128)(2,1)S(1)}, f32[8,32,128]{2,1,0:T(8,128)S(1)}) custom-call(bf16[2,256,128]{2,1,0:T(8,128)(2,1)S(1)} %get-tuple-element.6.patch, f32[256,128]{1,0:T(8,128)S(1)} %get-tuple-element.7.pgrad), custom_call_target="tpu_custom_call" | custom-call | tf_op jit(solution)/shard_map/pallas_call | solution.py:585
  57.6 5.9 %shard_map.81 = f32[24,256,64]{2,1,0:T(8,128)S(1)} custom-call(s32[32,2]{1,0:T(8,128)S(1)} %copy.18.off, s32[32,6]{1,0:T(8,128)S(1)} %copy.19.tmap, bf16[2,4,8,256,128]{4,3,2,1,0:T(8,128)(2,1)S(1)} %get-tuple-element.8.got), custom_call_target="tpu_custom_call" | custom-call | tf_op jit(solution)/shard_map/pallas_call | solution.py:602
  63.5 2.2 %reshape.14 = f32[24,4,4096]{2,1,0:T(4,128)} reshape(f32[24,256,64]{2,1,0:T(8,128)S(1)} %shard_map.81) | data formatting | bytes 3145728 | tf_op jit(solution)/shard_map/reshape | solution.py:609
  65.7 0.7 copy.21
Async XLA Ops:
  0.6 16.7 %copy-start = (bf16[8,256,256]{2,1,0:T(8,128)(2,1)S(1)}, bf16[8,256,256]{2,1,0:T(8,128)(2,1)}, u32[]{:S(2)}) copy-start(bf16[8,256,256]{2,1,0:T(8,128)(2,1)} %constant.2.clone.tables) | copy-start | bytes 3145732
  0.6 16.7 %copy-start.2 = (f32[1,128,128]{2,1,0:T(8,128)S(1)}, f32[1,128,128]{2,1,0:T(8,128)}, u32[]{:S(2)}) copy-start(f32[1,128,128]{2,1,0:T(8,128)} %intens.1) | copy-start | bytes 196612
  0.7 16.7 %copy-start.1 = (f32[2,128,128]{2,1,0:T(8,128)S(1)}, f32[2,128,128]{2,1,0:T(8,128)}, u32[]{:S(2)}) copy-start(f32[2,128,128]{2,1,0:T(8,128)} %probe.1) | copy-start | bytes 393220

commit v3 on v2

--- a/solution.py
+++ b/solution.py
@@ -165,75 +165,64 @@
 SM = pltpu.SMEM
 
 
-def one_hot(rows, cols, shift):
-    row = lax.broadcasted_iota(jnp.int32, (rows, cols), 0)
-    col = lax.broadcasted_iota(jnp.int32, (rows, cols), 1)
-    return jnp.where(col == row + shift, 1.0, 0.0).astype(jnp.bfloat16)
+HALF = TS // 2
+
+
+def indices(rows, cols):
+    return (
+        lax.broadcasted_iota(jnp.int32, (rows, cols), 0),
+        lax.broadcasted_iota(jnp.int32, (rows, cols), 1),
+    )
+
+
+def ones_at(where):
+    return jnp.where(where, 1.0, 0.0).astype(jnp.bfloat16)
+
+
+def stored_row(index):
+    return 2 * lax.rem(index, HALF) + lax.div(index, HALF)
 
 
 def bdot(a, b):
     return jnp.dot(a, b, preferred_element_type=jnp.float32)
 
 
-def class_of(tmap, me, per):
-    found = jnp.int32(0)
-    for r in range(OWN_R):
-        found = jnp.where(lax.div(tmap[r, 0], per) == me, r, found)
-    return found
-
-
-def place(off, n, rho):
-    y = off[n, 0]
-    x = off[n, 1]
-    ty = lax.div(y, TS)
-    tx = lax.div(x, TS)
-    step = lax.rem(rho - ty + 64 * OWN_R, OWN_R)
-    return ty + step, tx, x - tx * TS, step < 3
-
-
-def pack_kernel(owners, layers, per, off, tmap, tiles, slots):
-    me = lax.axis_index("pos")
-    z = lax.axis_index("tile")
-    rho = class_of(tmap, me, per)
-    for p in range(owners):
-        row, tx, ix, live = place(off, p * layers + z, rho)
-
-        @pl.when(live)
-        def _():
-            acc = None
-            for j in range(3):
-                local = tmap[row, tx + j] - me * per
-                part = bdot(tiles[local], one_hot(TS, 2 * TS, TS * j - ix))
-                acc = part if acc is None else acc + part
-            slots[p] = acc.astype(jnp.bfloat16)
-
-
-def fetch_kernel(owners, slots, got, send_sem, recv_sem, own_sem):
-    me = lax.axis_index("pos")
-    z = lax.axis_index("tile")
-    barrier = pltpu.get_barrier_semaphore()
-    for d in range(1, owners):
-        peer = lax.rem(me + d, owners)
-        pl.semaphore_signal(barrier, inc=1, device_id=(peer, z), device_id_type=MESH)
-    own = pltpu.make_async_copy(slots.at[me], got.at[me], own_sem)
-    own.start()
-    pl.semaphore_wait(barrier, owners - 1)
-    copies = []
-    for d in range(1, owners):
-        peer = lax.rem(me + d, owners)
-        copy = pltpu.make_async_remote_copy(
-            src_ref=slots.at[peer],
-            dst_ref=got.at[me],
-            send_sem=send_sem.at[d],
-            recv_sem=recv_sem.at[d],
-            device_id=(peer, z),
-            device_id_type=MESH,
-        )
-        copy.start()
-        copies.append(copy)
-    own.wait()
-    for copy in copies:
-        copy.wait()
+class Maps:
+    def __init__(self, offsets, tile_map):
+        self.offsets, self.tile_map = offsets, tile_map
+
+    def corner(self, n):
+        return self.offsets[0, n], self.offsets[1, n]
+
+    def tile(self, row, col):
+        return self.tile_map[col, row]
+
+    def class_of(self, me, per):
+        found = jnp.int32(0)
+        for r in range(OWN_R):
+            found = jnp.where(lax.div(self.tile(r, 0), per) == me, r, found)
+        return found
+
+    def place(self, n, rho):
+        y, x = self.corner(n)
+        ty = lax.div(y, TS)
+        tx = lax.div(x, TS)
+        step = lax.rem(rho - ty + 64 * OWN_R, OWN_R)
+        return ty + step, tx, x - tx * TS, step < 3
+
+
+def crop(maps, n, rho, me, per, rows, tiles):
+    row, tx, ix, _ = maps.place(n, rho)
+    row = jnp.minimum(row, rows - 1)
+    r, c = indices(2 * TS, 4 * TS)
+    same_parity = lax.div(r, TS) == lax.div(c, 2 * TS)
+    px, q = lax.rem(r, TS), lax.rem(c, 2 * TS)
+    acc = None
+    for j in range(3):
+        local = jnp.clip(maps.tile(row, tx + j) - me * per, 0, per - 1)
+        part = bdot(tiles[local], ones_at(same_parity & (q == px + (TS * j - ix))))
+        acc = part if acc is None else acc + part
+    return acc.astype(jnp.bfloat16)
 
 
 def split(a):
@@ -258,18 +247,19 @@
     return out[:width], out[width:]
 
 
-def wave_kernel(layers, per, off, tmap, got, probe, intens, tables, patch_out, pgrad):
-    n = lax.axis_index("pos") * layers + lax.axis_index("tile")
-    y = off[n, 0]
+def wave(maps, n, per, got, probe, intens, tables, keep, exit_done):
+    y, _ = maps.corner(n)
     ty = lax.div(y, TS)
     iy = y - ty * TS
     w = probe.shape[-1]
-    owner = [lax.div(tmap[ty + s, 0], per) for s in range(3)]
     rows = []
     for s in range(3):
-        block = got[owner[s]]
-        rows.append(jnp.concatenate([block[k * TS : (k + 1) * TS] for k in range(4)], axis=1))
-    patch = bdot(one_hot(w, 3 * TS, iy), jnp.concatenate(rows, axis=0))
+        block = got[lax.div(maps.tile(ty + s, 0), per)]
+        for half in (block[:, :w], block[:, w:]):
+            rows.append(jnp.concatenate([half[k * HALF : (k + 1) * HALF] for k in range(4)], axis=1))
+    r, c = indices(w, 3 * TS)
+    picks = ones_at(r + iy == lax.div(c, TS) * TS + stored_row(lax.rem(c, TS)))
+    patch = bdot(picks, jnp.concatenate(rows, axis=0))
     en_re, en_im, ex_re, ex_im = (patch[:, k * w : (k + 1) * w] for k in range(4))
     pr, pi = probe[0], probe[1]
     fw, fc, aw, ac = ((tables[2 * i], tables[2 * i + 1]) for i in range(4))
@@ -279,20 +269,18 @@
     far_re, far_im = both_sides(re, im, fw, fc)
     excess = far_re * far_re + far_im * far_im - intens[0]
     bk_re, bk_im = both_sides(excess * far_re, excess * far_im, fc, fw)
-    gx_re, gx_im = product(sp_re, -sp_im, bk_re, bk_im)
+    keep(1, *product(sp_re, -sp_im, bk_re, bk_im))
+    exit_done()
     re, im = product(ex_re, -ex_im, bk_re, bk_im)
     in_re, in_im = both_sides(re, im, ac, aw)
-    ge_re, ge_im = product(pr, -pi, in_re, in_im)
-    gp_re, gp_im = product(en_re, -en_im, in_re, in_im)
-    pgrad[0:w] = gp_re
-    pgrad[w : 2 * w] = gp_im
-    for k, part in enumerate((ge_re, ge_im, gx_re, gx_im)):
-        patch_out[k // 2, (k % 2) * w : (k % 2 + 1) * w, :] = part.astype(jnp.bfloat16)
-
-
-def spread_kernel(
-    owners, layers, patch, pgrad, got, ptotal, part, summed, layer_part,
-    own_sem, l_send, l_recv, z_send, z_recv, c_send, c_recv,
+    keep(0, *product(pr, -pi, in_re, in_im))
+    return product(en_re, -en_im, in_re, in_im)
+
+
+def main_kernel(
+    owners, layers, per, rows, offsets, tile_map, tiles, probe, intens, tables, got, ptotal,
+    slots, fetched, pgrad, part, summed, layer_part,
+    f_send, f_recv, l_send, l_recv, z_send, z_recv, c_send, c_recv,
     p_send, p_recv, q_send, q_recv, r_send, r_recv,
 ):
     me = lax.axis_index("pos")
@@ -304,7 +292,9 @@
     same = [m + core for m in mates]
     other = [m + 1 - core for m in mates]
     chunk = pgrad.shape[0] // owners
-    half = patch.shape[1] // 2
+    w = probe.shape[-1]
+    half = w
+    maps = Maps(offsets, tile_map)
 
     def remote(src, dst, ssem, rsem, p, t):
         return pltpu.make_async_remote_copy(
@@ -321,9 +311,16 @@
         pl.semaphore_signal(
             barrier, inc=1, device_id=(me, lax.rem(z + d, layers)), device_id_type=MESH
         )
-    own = pltpu.make_async_copy(patch, got.at[:, z, me], own_sem)
-    own.start()
-    pl.semaphore_wait(barrier, owners + layers - 2)
+    rho = maps.class_of(me, per)
+    fetches = []
+    for d in range(1, owners):
+        peer = lax.rem(me + d, owners)
+        slots[d] = crop(maps, peer * layers + z, rho, me, per, rows, tiles)
+        if d == 1:
+            pl.semaphore_wait(barrier, owners + layers - 2)
+        fetches.append(remote(slots.at[d], fetched.at[me], f_send.at[d], f_recv.at[d], peer, z))
+        fetches[-1].start()
+    fetched[me] = crop(maps, me * layers + z, rho, me, per, rows, tiles)
 
     def item(h, t, p, rows=None):
         ref = got.at[h, t, p]
@@ -371,6 +368,62 @@
         def _():
             climb(h, 1, 0, i, z, z - 1).start()
 
+    def sides(h, t):
+        arrived(h, t, 1).wait_recv()
+        corner(h, t, 0, 1, 2).start()
+        hand(h, t, 1).start()
+        if h == 0:
+            leave(0, 1)
+        arrived(h, t, 2).wait_recv()
+        corner(h, t, 1, 2, 1).start()
+        hand(h, t, 2).start()
+        if h == 0:
+            leave(0, 2)
+
+    def last(h, t):
+        corner_in(h, t, 0).wait_recv()
+        corner_in(h, t, 1).wait_recv()
+        hand(h, t, 3).start()
+        if h == 0:
+            leave(0, 3)
+
+    def step_z(h, t, i):
+        for way, layer, there in ((0, z - 1 - t, z + 1), (1, z + 1 + t, z - 1)):
+            @pl.when((layer >= 0) & (layer <= layers - 1))
+            def _():
+                climb(h, way, t, i, layer, there).wait_recv()
+                if t < layers - 2:
+
+                    @pl.when((there >= 0) & (there <= layers - 1))
+                    def _():
+                        climb(h, way, t + 1, i, layer, there).start()
+
+                hand(h, layer, i).start()
+                if h == 1:
+                    across(1, layer, 1).start()
+                    across(1, layer, 2).start()
+
+    def keep(h, re, im):
+        got[h, z, me, 0:w] = re.astype(jnp.bfloat16)
+        got[h, z, me, w : 2 * w] = im.astype(jnp.bfloat16)
+
+    def exit_done():
+        leave(1, 0)
+        across(1, z, 1).start()
+        across(1, z, 2).start()
+        hand(1, z, 0).start()
+
+    for copy in fetches:
+        copy.wait_recv()
+    gp_re, gp_im = wave(
+        maps, me * layers + z, per, fetched, probe, intens, tables, keep, exit_done
+    )
+    across(0, z, 1).start()
+    across(0, z, 2).start()
+    leave(0, 0)
+    hand(0, z, 0).start()
+    pgrad[0:w] = gp_re
+    pgrad[w : 2 * w] = gp_im
     probes = []
     for d in range(1, owners):
         peer = lax.rem(me + d, owners)
@@ -381,16 +434,8 @@
             )
         )
         probes[-1].start()
-    own.wait()
-    across(0, z, 1).start()
-    across(0, z, 2).start()
-    leave(1, 0)
-    leave(0, 0)
-    across(1, z, 1).start()
-    across(1, z, 2).start()
-    hand(0, z, 0).start()
-    hand(1, z, 0).start()
-
+    sides(0, z)
+    step_z(1, 0, 0)
     part[me] = pgrad[pl.ds(pl.multiple_of(me * chunk, chunk), chunk)]
     for copy in probes:
         copy.wait()
@@ -406,43 +451,6 @@
         )
         zs[-1].start()
 
-    def sides(h, t):
-        arrived(h, t, 1).wait_recv()
-        corner(h, t, 0, 1, 2).start()
-        hand(h, t, 1).start()
-        if h == 0:
-            leave(0, 1)
-        arrived(h, t, 2).wait_recv()
-        corner(h, t, 1, 2, 1).start()
-        hand(h, t, 2).start()
-        if h == 0:
-            leave(0, 2)
-
-    def last(h, t):
-        corner_in(h, t, 0).wait_recv()
-        corner_in(h, t, 1).wait_recv()
-        hand(h, t, 3).start()
-        if h == 0:
-            leave(0, 3)
-
-    def step_z(h, t, i):
-        for way, layer, there in ((0, z - 1 - t, z + 1), (1, z + 1 + t, z - 1)):
-            @pl.when((layer >= 0) & (layer <= layers - 1))
-            def _():
-                climb(h, way, t, i, layer, there).wait_recv()
-                if t < layers - 2:
-
-                    @pl.when((there >= 0) & (there <= layers - 1))
-                    def _():
-                        climb(h, way, t + 1, i, layer, there).start()
-
-                hand(h, layer, i).start()
-                if h == 1:
-                    across(1, layer, 1).start()
-                    across(1, layer, 2).start()
-
-    sides(0, z)
-    step_z(1, 0, 0)
     last(0, z)
     for copy in zs:
         copy.wait()
@@ -472,6 +480,8 @@
 
     for copy in outs:
         copy.wait()
+    for copy in fetches:
+        copy.wait_send()
 
     @pl.loop(0, layers)
     def _(t):
@@ -503,27 +513,40 @@
                     climb(0, way, t, i, layer, there).wait_send()
 
 
-def add_kernel(owners, layers, per, off, tmap, got, out):
+def add_kernel(owners, layers, per, offsets, tile_map, got, out):
     me = lax.axis_index("pos")
-    rho = class_of(tmap, me, per)
+    maps = Maps(offsets, tile_map)
+    rho = maps.class_of(me, per)
+    w = 2 * TS
     out[...] = jnp.zeros_like(out)
 
     @pl.loop(0, owners * layers)
     def _(n):
-        row, tx, ix, live = place(off, n, rho)
+        row, tx, ix, live = maps.place(n, rho)
 
         @pl.when(live)
         def _():
-            w = 2 * TS
-            pick_rows = one_hot(TS, w, row * TS - off[n, 0])
+            r, c = indices(TS, w)
+            picks = ones_at(c == stored_row(r) + (row * TS - maps.corner(n)[0]))
             t, p = lax.rem(n, layers), lax.div(n, layers)
             first, second = got[0, t, p], got[1, t, p]
             wide = jnp.concatenate([first[:w], first[w:], second[:w], second[w:]], axis=1)
-            rows = bdot(pick_rows, wide).astype(jnp.bfloat16)
-            block = jnp.concatenate([rows[:, k * w : (k + 1) * w] for k in range(4)], axis=0)
+            rows = bdot(picks, wide).astype(jnp.bfloat16)
+            block = jnp.concatenate(
+                [
+                    jnp.concatenate(
+                        [rows[:HALF, k * w : (k + 1) * w], rows[HALF:, k * w : (k + 1) * w]], axis=1
+                    )
+                    for k in range(4)
+                ],
+                axis=0,
+            )
+            r, c = indices(2 * w, w)
+            same_parity = lax.div(r, w) == lax.div(c, TS)
+            q, px = lax.rem(r, w), lax.rem(c, TS)
             for j in range(3):
-                local = tmap[row, tx + j] - me * per
-                out[local] += bdot(block, one_hot(w, TS, ix - TS * j))
+                local = maps.tile(row, tx + j) - me * per
+                out[local] += bdot(block, ones_at(same_parity & (q == px + (TS * j - ix))))
 
 
 def spectral_blocks(width):
@@ -553,59 +576,36 @@
     vm = pl.BlockSpec(memory_space=VM)
     sm = pl.BlockSpec(memory_space=SM)
     dma = pltpu.SemaphoreType.DMA
-    tiles = obj_tiles.reshape(per, 4 * TS, TS)
-    slot_shape = jax.ShapeDtypeStruct((owners, 4 * TS, w), bf)
-    slots = pl.pallas_call(
-        functools.partial(pack_kernel, owners, layers, per),
-        out_shape=slot_shape,
-        in_specs=[sm, sm, vm],
-        out_specs=vm,
-        compiler_params=params(),
-    )(offsets, tile_map, tiles)
-    got = pl.pallas_call(
-        functools.partial(fetch_kernel, owners),
-        out_shape=slot_shape,
-        in_specs=[vm],
-        out_specs=vm,
-        scratch_shapes=[dma((owners,)), dma((owners,)), dma],
-        compiler_params=params(collective_id=0, has_side_effects=True),
-    )(slots)
+    scalars = (offsets.T, tile_map.T)
+    tiles = obj_tiles.reshape(per, 4 * HALF, 2 * TS)
     tables = jnp.asarray(spectral_blocks(w))
-    grads, pgrad = pl.pallas_call(
-        functools.partial(wave_kernel, layers, per),
-        out_shape=[
-            jax.ShapeDtypeStruct((2, 2 * w, w), bf),
-            jax.ShapeDtypeStruct((2 * w, w), f32),
-        ],
-        in_specs=[sm, sm, vm, vm, vm, vm],
-        out_specs=[vm, vm],
-        compiler_params=params(),
-    )(offsets, tile_map, got, probe, intens, tables)
     chunk = 2 * w // owners
-    spread, ptotal = pl.pallas_call(
-        functools.partial(spread_kernel, owners, layers),
+    gathered, ptotal = pl.pallas_call(
+        functools.partial(main_kernel, owners, layers, per, tile_map.shape[0]),
         out_shape=[
             jax.ShapeDtypeStruct((2, layers, owners, 2 * w, w), bf),
             jax.ShapeDtypeStruct((owners, chunk, w), f32),
         ],
-        in_specs=[vm, vm],
+        in_specs=[sm, sm, vm, vm, vm, vm],
         out_specs=[vm, vm],
         scratch_shapes=[
-            VM((owners, chunk, w), f32), VM((chunk, w), f32), VM((layers, chunk, w), f32), dma,
+            VM((owners, 2 * TS, 2 * w), bf), VM((owners, 2 * TS, 2 * w), bf), VM((2 * w, w), f32),
+            VM((owners, chunk, w), f32), VM((chunk, w), f32), VM((layers, chunk, w), f32),
+            dma((owners,)), dma((owners,)),
             dma((2, layers, 4)), dma((2, layers, 4)),
             dma((2, 2, layers, 4)), dma((2, 2, layers, 4)),
             dma((2, layers, 4)), dma((2, layers, 4)),
             dma((owners,)), dma((owners,)), dma((layers,)), dma((layers,)), dma((owners,)), dma((owners,)),
         ],
-        compiler_params=params(collective_id=1, has_side_effects=True),
-    )(grads, pgrad)
+        compiler_params=params(collective_id=0, has_side_effects=True),
+    )(*scalars, tiles, probe, intens, tables)
     total = pl.pallas_call(
         functools.partial(add_kernel, owners, layers, per),
-        out_shape=jax.ShapeDtypeStruct((per, 4 * TS, TS), f32),
+        out_shape=jax.ShapeDtypeStruct((per, 4 * HALF, 2 * TS), f32),
         in_specs=[sm, sm, vm],
         out_specs=vm,
         compiler_params=params(),
-    )(offsets, tile_map, spread)
+    )(*scalars, gathered)
     return (total.reshape(per, 4, TS * TS), ptotal.reshape(2, w, w))
 
 

time: 66.9 us -> 62.8 us (0.939)
  local copies, waits for them, and re-layouts: 7.16 us -> 4.54 us
  Pallas kernels: 58.5 us -> 56.8 us
    unnamed x9 -> x11, local copies, waits for them, and re-layouts: 2.29 us -> 0.68 us
    pallas_call x4 -> x1, Pallas kernels: 52.5 us -> 51.5 us  [row_plan(): pl.pallas_call(functools.partial(main_kernel, owners, layers, per, tile_m...]
where the time goes in v3:
time: 62.8 us; the launch traced here: 62.1 us
  Pallas kernels  56.8 us (90%)
  local copies, waits for them, and re-layouts  4.54 us (7%)
  between operations  0.73 us (1%)
    pallas_call x1, Pallas kernels, row_plan(): pl.pallas_call(functools.partial(main_kernel, owners, layers, per, tile_m...  51.5 us
    pallas_call x1, Pallas kernels, row_plan(): pl.pallas_call(functools.partial(add_kernel, owners, layers, per), out_sh...  5.38 us
    reshape x1, local copies, waits for them, and re-layouts, row_plan(): tiles = obj_tiles.reshape(per, 4 * HALF, 2 * TS)  2.2 us
    reshape x1, local copies, waits for them, and re-layouts, row_plan(): return (total.reshape(per, 4, TS * TS), ptotal.reshape(2, w, w))  1.67 us

profile of v3, /device:TPU:0, one launch (start us, length us, event | category | flops | bytes accessed | tf_op | source)
XLA Modules:
  0.0 62.1 jit_solution(11756330906191332507)
XLA Ops:
  0.6 0.0 copy-start
  0.6 0.0 copy-start.2
  0.7 0.0 copy-start.1
  0.7 0.0 copy-start.4
  0.7 0.0 copy-start.3
  0.7 2.2 %reshape.13.tiles = bf16[24,128,128]{2,1,0:T(8,128)(2,1)S(1)} reshape(bf16[24,4,4096]{2,1,0:T(4,128)(2,1)} %param.6) | data formatting | bytes 1572864 | tf_op jit(solution)/shard_map/reshape | solution.py:580
  2.9 0.0 copy-done
  2.9 0.0 copy-done.2
  2.9 0.0 copy-done.1
  2.9 0.0 copy-done.4
  2.9 0.0 copy-done.3
  2.9 51.5 %shard_map.77 = (bf16[2,4,8,256,128]{4,3,2,1,0:T(8,128)(2,1)S(1)}, f32[8,32,128]{2,1,0:T(8,128)S(1)}) custom-call(s32[2,32]{1,0:T(2,128)S(1)} %bitcast.6, s32[6,32]{1,0:T(8,128)S(1)} %bitcast.4, bf16[24,128,128]{2,1,0:T(8,128)(2,1)S(1)} %reshape.13.tiles, f32[2,128,128]{2,1,0:T(8,128)S(1)} %copy-done.1, f32[1,128,128]{2,1,0:T(8,128)S(1)} %copy-done.2, ...), custom_call_target="tpu_custom_call" | custom-call | tf_op jit(solution)/shard_map/pallas_call | solution.py:583
  54.4 5.4 %shard_map.78 = f32[24,128,128]{2,1,0:T(8,128)S(1)} custom-call(s32[2,32]{1,0:T(2,128)S(1)} %bitcast.7, s32[6,32]{1,0:T(8,128)S(1)} %bitcast.5, bf16[2,4,8,256,128]{4,3,2,1,0:T(8,128)(2,1)S(1)} %get-tuple-element.4.got), custom_call_target="tpu_custom_call" | custom-call | tf_op jit(solution)/shard_map/pallas_call | solution.py:602
  59.8 1.7 %reshape.14 = f32[24,4,4096]{2,1,0:T(4,128)} reshape(f32[24,128,128]{2,1,0:T(8,128)S(1)} %shard_map.78) | data formatting | bytes 3145728 | tf_op jit(solution)/shard_map/reshape | solution.py:609
  61.5 0.7 %copy.9 = f32[2,128,128]{2,1,0:T(8,128)} copy(f32[2,128,128]{2,1,0:T(8,128)S(1)} %bitcast.3) | data formatting | bytes 262144
Async XLA Ops:
  0.6 2.3 %copy-start = (bf16[8,256,256]{2,1,0:T(8,128)(2,1)S(1)}, bf16[8,256,256]{2,1,0:T(8,128)(2,1)}, u32[]{:S(2)}) copy-start(bf16[8,256,256]{2,1,0:T(8,128)(2,1)} %constant.2.clone.tables) | copy-start | bytes 3145732
  0.6 2.3 %copy-start.2 = (f32[1,128,128]{2,1,0:T(8,128)S(1)}, f32[1,128,128]{2,1,0:T(8,128)}, u32[]{:S(2)}) copy-start(f32[1,128,128]{2,1,0:T(8,128)} %intens.1) | copy-start | bytes 196612
  0.7 2.3 %copy-start.1 = (f32[2,128,128]{2,1,0:T(8,128)S(1)}, f32[2,128,128]{2,1,0:T(8,128)}, u32[]{:S(2)}) copy-start(f32[2,128,128]{2,1,0:T(8,128)} %probe.1) | copy-start | bytes 393220
  0.7 2.3 %copy-start.4 = (s32[32,2]{0,1:T(2,128)S(1)}, s32[32,2]{0,1:T(2,128)}, u32[]{:S(2)}) copy-start(s32[32,2]{0,1:T(2,128)} %param.8) | copy-start | bytes 772
  0.7 2.3 %copy-start.3 = (s32[32,6]{0,1:T(8,128)S(1)}, s32[32,6]{0,1:T(8,128)}, u32[]{:S(2)}) copy-start(s32[32,6]{0,1:T(8,128)} %param.7) | copy-start | bytes 2308
